TPU v7x, 256 devices: a whole 4x4x8 slice. The times are simulated.
256 devices in a mesh: group: 4 (over z_hi, core), fsdp: 64 (over y, x, z_lo).
Axes of the slice: x: 4, y: 4, z: 8 (z_hi: 2, z_lo: 4; z = z_hi * 4 + z_lo), core: 2. Of those that a mesh axis runs over, the one named last changes fastest.
Arguments:
- hidden_rows: bfloat16 [4, 32768, 4096], P('group', 'fsdp'), may hold values from -16 to 16
- out_grad: bfloat16 [4, 32768, 1024], P('group', 'fsdp'), may hold values from -6 to 6
- params: bfloat16 [4, 4096, 1024], P('group', 'fsdp'), may hold values from -3 to 3
- first_moment: bfloat16 [4, 4096, 1024], P('group', 'fsdp'), may hold values from -1.8 to 1.8
- second_moment: bfloat16 [4, 4096, 1024], P('group', 'fsdp'), may hold values from 0.099609375 to 2
- anchor: bfloat16 [4096, 1024], P('fsdp', 'group'), may hold values from -2 to 2
- outer_momentum: bfloat16 [4096, 1024], P('fsdp', 'group'), may hold values from -4 to 4
Outputs:
- layer_out: bfloat16 [4, 32768, 1024], P('group', 'fsdp')
- input_grad: bfloat16 [4, 32768, 4096], P('group', 'fsdp')
- new_params: bfloat16 [4096, 1024], P('fsdp')
- new_first: bfloat16 [4, 4096, 1024], P('group', 'fsdp')
- new_second: bfloat16 [4, 4096, 1024], P('group', 'fsdp')
- new_momentum: bfloat16 [4096, 1024], P('fsdp', 'group')
All inputs are finite; a program needn't handle non-finite values.
Results may differ from a plain program's by a relative error of at most 0.001.
Values may be sent and summed in bfloat16 or wider, within the bound.
A program may use at most 128 MiB of HBM per device.

v0:
```python
import jax
import jax.numpy as jnp
from jax import lax
from jax.sharding import PartitionSpec as P

D = 1024
FF = 4096


beta_first = 0.9
beta_second = 0.95
adam_eps = 1e-08
learn_rate = 0.1
decay_rate = 0.1
outer_rate = 0.7
outer_beta = 0.9


def local(hidden_rows, out_grad, params, first_moment, second_moment, anchor, outer_momentum):
    hidden = hidden_rows[0]
    weight = params[0]
    cotangent = out_grad[0]
    token_count = hidden.shape[0]
    token_total = token_count * lax.axis_size("fsdp")
    scale_forward = FF ** (-0.5)
    scale_backward = D ** (-0.5)
    scale_gradient = token_total ** (-0.5)
    columns = hidden
    forward = jnp.dot(
        columns,
        lax.all_gather(weight, "fsdp", axis=0, tiled=True),
        preferred_element_type=jnp.float32,
    )
    backward = lax.dot_general(
        cotangent,
        lax.all_gather(weight, "fsdp", axis=0, tiled=True),
        (((1,), (1,)), ((), ())),
        preferred_element_type=jnp.float32,
    )
    layer_out = (forward * scale_forward).astype(jnp.bfloat16)[None]
    input_grad = (backward * scale_backward).astype(jnp.bfloat16)[None]
    columns = hidden
    gradient = (
        lax.psum_scatter(
            lax.dot_general(
                columns, cotangent, (((0,), (0,)), ((), ())), preferred_element_type=jnp.float32
            ),
            "fsdp",
            scatter_dimension=0,
            tiled=True,
        )
        * scale_gradient
    )
    first_new = beta_first * first_moment[0].astype(jnp.float32) + (1.0 - beta_first) * gradient
    second_new = (
        beta_second * second_moment[0].astype(jnp.float32)
        + (1.0 - beta_second) * gradient * gradient
    )
    weight_full = weight.astype(jnp.float32)
    inner_params = weight_full - learn_rate * (
        first_new / (jnp.sqrt(second_new) + adam_eps) + decay_rate * weight_full
    )
    group_count = lax.axis_size("group")
    summed = lax.psum_scatter(inner_params, "group", scatter_dimension=1, tiled=True)
    anchor_full = anchor.astype(jnp.float32)
    pseudo_grad = anchor_full - summed / group_count
    momentum = outer_beta * outer_momentum.astype(jnp.float32) + pseudo_grad
    new_share = (anchor_full - outer_rate * (pseudo_grad + outer_beta * momentum)).astype(
        jnp.bfloat16
    )
    new_params = lax.all_gather(new_share, "group", axis=1, tiled=True)
    new_momentum = momentum.astype(jnp.bfloat16)
    return (
        layer_out,
        input_grad,
        new_params,
        first_new.astype(jnp.bfloat16)[None],
        second_new.astype(jnp.bfloat16)[None],
        new_momentum,
    )


def solution(mesh):
    return jax.shard_map(
        local,
        mesh=mesh,
        in_specs=(
            P("group", "fsdp", None),
            P("group", "fsdp", None),
            P("group", "fsdp", None),
            P("group", "fsdp", None),
            P("group", "fsdp", None),
            P("fsdp", "group"),
            P("fsdp", "group"),
        ),
        out_specs=(
            P("group", "fsdp", None),
            P("group", "fsdp", None),
            P("fsdp", None),
            P("group", "fsdp", None),
            P("group", "fsdp", None),
            P("fsdp", "group"),
        ),
        check_vma=False,
    )
```

profile of v0, /device:TPU:1, one launch (start us, length us, event | category | flops | bytes accessed | tf_op | source)
XLA Modules:
  0.0 877.7 jit_solution(657754159526740561)
XLA Ops:
  7.2 0.0 copy-start
  7.2 0.0 all-gather.3.cloned.1.call-start
  7.2 0.7 all-gather.3.cloned.1.call-update
  7.9 0.0 reduce-scatter.3.cloned.1.call-start
  8.0 0.4 copy-done
  8.4 10.3 %fusion.9 = f32[4096,1024]{1,0:T(8,128)} fusion(bf16[1,512,4096]{2,1,0:T(8,128)(2,1)} %param.7, bf16[1,512,1024]{2,1,0:T(8,128)(2,1)S(1)} %copy-done), kind=kOutput, calls=%fused_computation.6 | convolution fusion | flops 4294967296 | bytes 22020096 | tf_op jit(solution)/shard_map/dot_general | solution.py:45
  18.7 0.0 reduce-scatter.3.cloned.1.call-update
  18.8 0.0 copy-start.1
  18.8 0.0 copy-start.2
  18.8 0.0 copy-start.3
  18.8 0.0 reduce-scatter.5.cloned.1.call-start
  18.9 331.0 %all-gather.3.cloned.1.call-done = bf16[1,4096,1024]{2,1,0:T(8,128)(2,1)} async-done(((bf16[1,64,1024]{2,1,0:T(8,128)(2,1)}), bf16[1,4096,1024]{2,1,0:T(8,128)(2,1)}) %all-gather.3.cloned.1.call-update) | async-done | bytes 8388624 | tf_op jit(solution)/shard_map/all_gather | solution.py:31
  349.8 10.1 %fusion.16 = bf16[1,512,1024]{2,1,0:T(8,128)(2,1)} fusion(bf16[1,4096,1024]{2,1,0:T(8,128)(2,1)} %all-gather.3.cloned.1.call-done, bf16[1,512,4096]{2,1,0:T(8,128)(2,1)} %param.7), kind=kOutput, calls=%fused_computation.10 | convolution fusion | flops 4296015872 | bytes 13631488 | tf_op jit(solution)/shard_map/dot_general | solution.py:29
  360.0 418.7 %reduce-scatter.3.cloned.1.call-done = f32[64,1024]{1,0:T(8,128)} async-done(((f32[4096,1024]{1,0:T(8,128)}), f32[64,1024]{1,0:T(8,128)}) %reduce-scatter.3.cloned.1.call-update) | async-done | bytes 262160 | tf_op jit(solution)/shard_map/reduce_scatter | solution.py:44
  778.7 0.0 copy-done.1
  778.7 0.0 copy-done.2
  778.7 0.0 copy-done.3
  778.7 2.0 convert_bitcast_fusion
  780.7 0.0 reduce-scatter.5.cloned.1.call-update
  780.7 0.0 copy-start.4
  780.7 0.0 copy-start.5
  780.7 9.5 %fusion.6 = bf16[1,512,4096]{2,1,0:T(8,128)(2,1)} fusion(bf16[1,4096,1024]{2,1,0:T(8,128)(2,1)} %all-gather.3.cloned.1.call-done, bf16[1,512,1024]{2,1,0:T(8,128)(2,1)S(1)} %copy-done), kind=kOutput, calls=%fused_computation.5 | convolution fusion | flops 4299161600 | bytes 13631488 | tf_op jit(solution)/shard_map/dot_general | solution.py:34
  790.2 68.9 %reduce-scatter.5.cloned.1.call-done = f32[64,256]{1,0:T(8,128)} async-done(((f32[64,1024]{1,0:T(8,128)}), f32[64,256]{1,0:T(8,128)}) %reduce-scatter.5.cloned.1.call-update) | async-done | bytes 65552 | tf_op jit(solution)/shard_map/reduce_scatter | solution.py:64
  859.1 0.0 copy-done.4
  859.1 0.0 copy-done.5
  859.1 1.5 fusion.28
  860.6 9.9 %all_gather.8 = bf16[64,1024]{1,0:T(8,128)(2,1)S(1)} all-gather(bf16[64,256]{1,0:T(8,128)(2,1)S(1)} %get-tuple-element.10), channel_id=1, replica_groups=mesh['group'=4,'fsdp'=64] {'group'}, dimensions={1}, use_global_device_ids=true | all-gather | bytes 163840 | tf_op jit(solution)/shard_map/all_gather | solution.py:71
  870.5 0.7 copy.14
Async XLA Ops:
  7.2 1.2 copy-start
  7.2 342.7 %all-gather.3.cloned.1.call-start = ((), (), s32[]{:S(2)}) async-start(), calls=%async_computation.4 | async-start | bytes 8519680 | tf_op jit(solution)/shard_map/all_gather | solution.py:31
  7.9 770.8 %reduce-scatter.3.cloned.1.call-start = ((), (), s32[]{:S(2)}) async-start(), calls=%async_computation.2 | async-start | bytes 17039360 | tf_op jit(solution)/shard_map/reduce_scatter | solution.py:44
  18.8 759.9 %copy-start.1 = (bf16[1,64,1024]{2,1,0:T(8,128)(2,1)S(1)}, bf16[1,64,1024]{2,1,0:T(8,128)(2,1)}, u32[]{:S(2)}) copy-start(bf16[1,64,1024]{2,1,0:T(8,128)(2,1)} %param.9) | copy-start | bytes 393220
  18.8 759.9 %copy-start.2 = (bf16[1,64,1024]{2,1,0:T(8,128)(2,1)S(1)}, bf16[1,64,1024]{2,1,0:T(8,128)(2,1)}, u32[]{:S(2)}) copy-start(bf16[1,64,1024]{2,1,0:T(8,128)(2,1)} %param.11) | copy-start | bytes 393220
  18.8 759.9 %copy-start.3 = (bf16[1,64,1024]{2,1,0:T(8,128)(2,1)S(1)}, bf16[1,64,1024]{2,1,0:T(8,128)(2,1)}, u32[]{:S(2)}) copy-start(bf16[1,64,1024]{2,1,0:T(8,128)(2,1)} %param.10) | copy-start | bytes 393220
  18.8 840.3 %reduce-scatter.5.cloned.1.call-start = ((), (), s32[]{:S(2)}) async-start(), calls=%async_computation.3 | async-start | bytes 327680 | tf_op jit(solution)/shard_map/reduce_scatter | solution.py:64
  780.7 78.4 %copy-start.4 = (bf16[64,256]{1,0:T(8,128)(2,1)S(1)}, bf16[64,256]{1,0:T(8,128)(2,1)}, u32[]{:S(2)}) copy-start(bf16[64,256]{1,0:T(8,128)(2,1)} %param.13) | copy-start | bytes 98308
  780.7 78.4 %copy-start.5 = (bf16[64,256]{1,0:T(8,128)(2,1)S(1)}, bf16[64,256]{1,0:T(8,128)(2,1)}, u32[]{:S(2)}) copy-start(bf16[64,256]{1,0:T(8,128)(2,1)} %param.12) | copy-start | bytes 98308
Sparse Core Ops, SparseCore 0:
  9.8 339.9 all-gather.2
  352.4 426.2 reduce-scatter.2
  781.4 77.6 reduce-scatter.4
where the time goes:
time: 878 us
  waiting for transfers between devices  819 us (93%)
  matrix products  29.9 us (3%)
  between operations  13.8 us (2%)
  blocking collectives  9.94 us (1%)
    reduce_scatter x1, waiting for transfers between devices, local(): lax.psum_scatter(lax.dot_general(columns, cotangent, (((0,), (0,)), ((),...  419 us
    all_gather x1, waiting for transfers between devices, local(): lax.all_gather(weight, 'fsdp', axis=0, tiled=True)  331 us
    reduce_scatter x1, waiting for transfers between devices, local(): lax.psum_scatter(inner_params, 'group', scatter_dimension=1, tiled=True)  68.9 us
  transfers between devices with their start and end apart: 3, of which 3 were waited for; matrix products, arithmetic and copies ran while one was open for 3% of the time, Pallas kernels for 0%

commit v1 on v0

v1 whole, which is shorter than its diff:
```python
import jax
import jax.numpy as jnp
from jax import lax
from jax.experimental import pallas as pl
from jax.experimental.pallas import tpu as pltpu
from jax.sharding import PartitionSpec as P

D = 1024
FF = 4096
TOKENS = 32768
BLOCK = 64
LOCAL = 512
CHUNKS = 4
ROWS = BLOCK // CHUNKS
HALF = D // 2
QUARTER = D // 4
MIB = 1 << 20

beta_first = 0.9
beta_second = 0.95
adam_eps = 1e-08
learn_rate = 0.1
decay_rate = 0.1
outer_rate = 0.7
outer_beta = 0.9

bf16 = jnp.bfloat16
f32 = jnp.float32


def kernel(
    h_hbm, g_hbm, w_hbm, fm, sm, an, om,
    lo_hbm, ig_hbm, np_out, nf_out, ns_out, nm_out,
    h, g, gr, wf, ht, htr, part, o1, n1, s1, sums, o2, n2, s2, plane, zin, inner, gin, share, lo, ig,
    in_sem, out_sem,
    wz_ss, wz_rs, ag_ss, ag_rs, ex_ss, ex_rs, r1_ss, r1_rs, r2_ss, r2_rs, zz_ss, zz_rs, gi_ss, gi_rs, np_ss, np_rs,
):
    me = lax.axis_index("fsdp")
    grp = lax.axis_index("group")
    z, x, y = lax.rem(me, 4), lax.rem(me // 4, 4), me // 16
    parity, level = lax.rem(z, 2), z // 2

    def at(xx, yy, zz):
        return {"fsdp": (yy * 4 + xx) * 4 + zz}

    def near(axis, step):
        if axis == 0:
            return at(lax.rem(x + step + 4, 4), y, z)
        return at(x, lax.rem(y + step + 4, 4), z)

    def peer(e):
        core, high = lax.rem(grp, 2), grp // 2
        core = 1 - core if e & 1 else core
        high = 1 - high if e & 2 else high
        return high * 2 + core

    def copy(src, dst, ss, rs, device):
        return pltpu.make_async_remote_copy(
            src_ref=src, dst_ref=dst, send_sem=ss, recv_sem=rs, device_id=device, device_id_type=pl.DeviceIdType.MESH
        )

    zpair = at(x, y, z + 1 - 2 * parity)
    zcross = at(x, y, lax.rem(z + 2, 4))
    steps = (1, -1)

    load_g = pltpu.make_async_copy(g_hbm, g, in_sem.at[0])
    load_h = pltpu.make_async_copy(h_hbm, h, in_sem.at[1])
    load_w = pltpu.make_async_copy(w_hbm, wf.at[y, x, z], in_sem.at[2])
    load_w.start()
    load_h.start()
    load_g.start()

    barrier = pltpu.get_barrier_semaphore()
    others = [near(a, s) for a in (0, 1) for s in steps]
    others += [at(x, y, lax.rem(z + r, 4)) for r in (1, 2, 3)]
    others += [{"group": peer(e)} for e in (1, 2, 3)]
    for other in others:
        pl.semaphore_signal(barrier, inc=1, device_id=other, device_id_type=pl.DeviceIdType.MESH)
    pl.semaphore_wait(barrier, len(others))

    def wz(r):
        return copy(w_hbm, wf.at[y, x, z], wz_ss.at[r - 1], wz_rs.at[r - 1], at(x, y, lax.rem(z + r, 4)))

    def gather(kind, r, hf, i):
        step = steps[i]
        zs = lax.rem(z + r, 4)
        cols = pl.ds(hf * HALF, HALF)
        first, second = hf, 1 - hf
        mine, across = (x, y) if hf == 0 else (y, x)
        prev = lax.rem(mine - step + 4, 4)
        back = lax.rem(across - step + 4, 4)
        if kind == 0:
            ref, axis = wf.at[y, x, zs, :, cols], first
        elif kind == 1:
            rows = pl.ds(i * (BLOCK // 2), BLOCK // 2)
            ref = wf.at[y, prev, zs, rows, cols] if hf == 0 else wf.at[prev, x, zs, rows, cols]
            axis = first
        elif kind == 2:
            ref = wf.at[y, :, zs, :, cols] if hf == 0 else wf.at[:, x, zs, :, cols]
            axis = second
        else:
            pair = pl.ds(2 * i, 2)
            ref = wf.at[back, pair, zs, :, cols] if hf == 0 else wf.at[pair, back, zs, :, cols]
            axis = second
        return copy(ref, ref, ag_ss.at[r, kind, hf, i], ag_rs.at[r, kind, hf, i], near(axis, step))

    def send_g():
        return copy(g_hbm, gr, ex_ss.at[CHUNKS], ex_rs.at[CHUNKS], zpair)

    def send_h(k):
        return copy(ht.at[1 - parity, k], htr.at[k], ex_ss.at[k], ex_rs.at[k], zpair)

    def chunk1(k, hf, dest, side):
        cols = pl.ds(hf * HALF, HALF)
        two = pl.ds(2 * side, 2)
        return part.at[k, two, dest, :, cols] if hf == 0 else part.at[k, dest, two, :, cols]

    def reduce1(kind, k, hf, i):
        step = steps[i]
        mine = x if hf == 0 else y
        if kind == 0:
            src, dst = chunk1(k, hf, lax.rem(mine + 2, 4), i), o1.at[k, hf, i]
        elif kind == 1:
            src, dst = chunk1(k, hf, lax.rem(mine + step + 4, 4), 1 - i), n1.at[k, hf, i]
        else:
            src, dst = o1.at[k, hf, i], s1.at[k, hf, i]
        return copy(src, dst, r1_ss.at[k, kind, hf, i], r1_rs.at[k, kind, hf, i], near(hf, step))

    def chunk2(k, hf, dest, side):
        return sums.at[k, hf, dest, pl.ds(side * ROWS, ROWS)]

    def reduce2(kind, k, hf, i):
        step = steps[i]
        mine = y if hf == 0 else x
        if kind == 0:
            src, dst = chunk2(k, hf, lax.rem(mine + 2, 4), i), o2.at[k, hf, i]
        elif kind == 1:
            src, dst = chunk2(k, hf, lax.rem(mine + step + 4, 4), 1 - i), n2.at[k, hf, i]
        else:
            src, dst = o2.at[k, hf, i], s2.at[k, hf, i]
        return copy(src, dst, r2_ss.at[k, kind, hf, i], r2_rs.at[k, kind, hf, i], near(1 - hf, step))

    def send_z(k):
        return copy(plane.at[k, 1 - level], zin.at[k], zz_ss.at[k], zz_rs.at[k], zcross)

    def send_inner(k, e):
        other = peer(e)
        return copy(
            inner.at[k, :, pl.ds(pl.multiple_of(other * QUARTER, QUARTER), QUARTER)],
            gin.at[k, e - 1], gi_ss.at[k, e - 1], gi_rs.at[k, e - 1], {"group": other},
        )

    def send_share(k, e):
        ref = share.at[k, :, pl.ds(pl.multiple_of(grp * QUARTER, QUARTER), QUARTER)]
        return copy(ref, ref, np_ss.at[k, e - 1], np_rs.at[k, e - 1], {"group": peer(e)})

    both = [(hf, i) for hf in (0, 1) for i in (0, 1)]

    def ga(r):
        for hf, i in both:
            gather(0, r, hf, i).start()

    def gb(r):
        for hf, i in both:
            gather(0, r, hf, i).wait_recv()
            gather(1, r, hf, i).start()

    def gc(r):
        for hf, i in both:
            gather(1, r, hf, i).wait_recv()
        for hf, i in both:
            gather(2, r, hf, i).start()

    def gd(r):
        for hf, i in both:
            gather(2, r, hf, i).wait_recv()
            gather(3, r, hf, i).start()

    def ge(r):
        for hf, i in both:
            gather(3, r, hf, i).wait_recv()

    def ra(k):
        @pl.loop(0, D // 256)
        def _(n):
            cols = pl.ds(pl.multiple_of(n * 256, 256), 256)
            mine = ht[parity, k].reshape(32 * ROWS, LOCAL)
            theirs = htr[k].reshape(32 * ROWS, LOCAL)
            total = jnp.dot(mine, g[:, cols], preferred_element_type=f32)
            total += jnp.dot(theirs, gr[:, cols], preferred_element_type=f32)
            part[k, :, :, :, cols] = total.reshape(4, 4, 2 * ROWS, 256)

        for kind in (0, 1):
            for hf, i in both:
                reduce1(kind, k, hf, i).start()

    def rb(k):
        for hf, i in both:
            mine = x if hf == 0 else y
            reduce1(0, k, hf, i).wait_recv()
            o1[k, hf, i] = o1[k, hf, i] + chunk1(k, hf, lax.rem(mine + steps[i] + 4, 4), i)[...]
            reduce1(2, k, hf, i).start()

    def rc(k):
        for hf in (0, 1):
            mine = x if hf == 0 else y
            for i in (0, 1):
                reduce1(1, k, hf, 1 - i).wait_recv()
                reduce1(2, k, hf, i).wait_recv()
                sums[k, hf, pl.ds(2 * i, 2)] = (chunk1(k, hf, mine, i)[...] + s1[k, hf, i]) + n1[k, hf, 1 - i]
        for kind in (0, 1):
            for hf, i in both:
                reduce2(kind, k, hf, i).start()

    def rd(k):
        for hf, i in both:
            mine = y if hf == 0 else x
            reduce2(0, k, hf, i).wait_recv()
            o2[k, hf, i] = o2[k, hf, i] + chunk2(k, hf, lax.rem(mine + steps[i] + 4, 4), i)[...]
            reduce2(2, k, hf, i).start()

    def re(k):
        for hf in (0, 1):
            mine = y if hf == 0 else x
            for i in (0, 1):
                reduce2(1, k, hf, 1 - i).wait_recv()
                reduce2(2, k, hf, i).wait_recv()
                plane[k, i, :, pl.ds(hf * HALF, HALF)] = (chunk2(k, hf, mine, i)[...] + s2[k, hf, i]) + n2[k, hf, 1 - i]
        send_z(k).start()

    def rf(k):
        send_z(k).wait_recv()
        rows = pl.ds(pl.multiple_of(k * ROWS, ROWS), ROWS)
        grad = (plane[k, level] + zin[k]) * (TOKENS ** (-0.5))
        first = beta_first * fm[rows, :].astype(f32) + (1.0 - beta_first) * grad
        second = beta_second * sm[rows, :].astype(f32) + (1.0 - beta_second) * grad * grad
        weight = wf[y, x, z, rows, :].astype(f32)
        nf_out[rows, :] = first.astype(bf16)
        ns_out[rows, :] = second.astype(bf16)
        inner[k] = weight - learn_rate * (first / (jnp.sqrt(second) + adam_eps) + decay_rate * weight)
        for e in (1, 2, 3):
            send_inner(k, e).start()

    def rg(k):
        rows = pl.ds(pl.multiple_of(k * ROWS, ROWS), ROWS)
        mine = pl.ds(pl.multiple_of(grp * QUARTER, QUARTER), QUARTER)
        total = inner[k, :, mine]
        for e in (1, 2, 3):
            send_inner(k, e).wait_recv()
            total += gin[k, e - 1]
        anchor = an[rows, :].astype(f32)
        pseudo = anchor - total / 4
        momentum = outer_beta * om[rows, :].astype(f32) + pseudo
        nm_out[rows, :] = momentum.astype(bf16)
        share[k, :, mine] = (anchor - outer_rate * (pseudo + outer_beta * momentum)).astype(bf16)
        for e in (1, 2, 3):
            send_share(k, e).start()

    def rh(k):
        for e in (1, 2, 3):
            send_share(k, e).wait_recv()
        np_out[pl.ds(pl.multiple_of(k * ROWS, ROWS), ROWS), :] = share[k]

    def out_lo(n):
        cols = pl.ds(pl.multiple_of(n * 256, 256), 256)
        return pltpu.make_async_copy(lo.at[:, cols], lo_hbm.at[:, cols], out_sem.at[0, n])

    def out_ig(n):
        cols = pl.ds(pl.multiple_of(n * 1024, 1024), 1024)
        return pltpu.make_async_copy(ig.at[:, cols], ig_hbm.at[:, cols], out_sem.at[1, n])

    def piece(n):
        cols = pl.ds(pl.multiple_of(n * 256, 256), 256)
        total = jnp.dot(h[...], wf[:, :, :, :, cols].reshape(FF, 256), preferred_element_type=f32)
        lo[:, cols] = (total * (FF ** (-0.5))).astype(bf16)
        out_lo(n).start()

        @pl.loop(0, 4)
        def _(c):
            units = pl.ds(pl.multiple_of(n * 1024 + c * 256, 256), 256)
            back = lax.dot_general(
                g[...], wf[n, c].reshape(256, D), (((1,), (1,)), ((), ())), preferred_element_type=f32
            )
            ig[:, units] = (back * (D ** (-0.5))).astype(bf16)

        out_ig(n).start()

    for r in (1, 2, 3):
        wz(r).start()
    load_w.wait()
    ga(0)
    load_h.wait()

    @pl.loop(0, 32)
    def _(n):
        d, m = n // 2, lax.rem(n, 2)
        turned = h[:, pl.ds(pl.multiple_of(n * 128, 128), 128)].T
        for par in (0, 1):
            ht[par, :, d, m] = turned[par * BLOCK : (par + 1) * BLOCK].reshape(CHUNKS, ROWS, LOCAL)

    gb(0)
    send_g().start()
    load_g.wait()

    @pl.loop(0, 4)
    def _(r):
        @pl.when(r < 3)
        def _():
            copy(w_hbm, wf.at[y, x, z], wz_ss.at[2 - r], wz_rs.at[2 - r], zpair).wait_recv()
            ga(r + 1)

        gc(r)
        send_h(r).start()

        @pl.when(r < 3)
        def _():
            gb(r + 1)

        gd(r)

    @pl.loop(0, 4)
    def _(r):
        ge(r)

    send_g().wait_recv()

    @pl.loop(0, CHUNKS + 4)
    def _(t):
        @pl.when(t < CHUNKS)
        def _():
            send_h(t).wait_recv()
            ra(t)

        @pl.when((t >= 1) & (t < CHUNKS + 1))
        def _():
            rc(t - 1)

        @pl.when((t >= 2) & (t < CHUNKS + 2))
        def _():
            rf(t - 2)

        @pl.when(t < CHUNKS)
        def _():
            piece(t)
            rb(t)

        @pl.when((t >= 1) & (t < CHUNKS + 1))
        def _():
            rd(t - 1)

        @pl.when((t >= 3) & (t < CHUNKS + 3))
        def _():
            rg(t - 3)

        @pl.when((t >= 1) & (t < CHUNKS + 1))
        def _():
            re(t - 1)

        @pl.when(t >= 4)
        def _():
            rh(t - 4)

    for r in (1, 2, 3):
        wz(r).wait_send()
    send_g().wait_send()

    @pl.loop(0, 4)
    def _(k):
        for hf, i in both:
            for kind in range(4):
                gather(kind, k, hf, i).wait_send()
            for kind in range(3):
                reduce1(kind, k, hf, i).wait_send()
                reduce2(kind, k, hf, i).wait_send()
        send_h(k).wait_send()
        send_z(k).wait_send()
        for e in (1, 2, 3):
            send_inner(k, e).wait_send()
            send_share(k, e).wait_send()
        out_lo(k).wait()
        out_ig(k).wait()


def local(hidden_rows, out_grad, params, first_moment, second_moment, anchor, outer_momentum):
    anywhere = pl.BlockSpec(memory_space=pl.ANY)
    vmem = pl.BlockSpec(memory_space=pltpu.VMEM)
    dma = pltpu.SemaphoreType.DMA
    n = CHUNKS
    step1 = pltpu.VMEM((n, 2, 2, 2, 2 * ROWS, HALF), f32)
    step2 = pltpu.VMEM((n, 2, 2, ROWS, HALF), f32)

    def pair(*shape):
        return [dma(shape), dma(shape)]

    out = pl.pallas_call(
        kernel,
        out_shape=[
            jax.ShapeDtypeStruct((LOCAL, D), bf16),
            jax.ShapeDtypeStruct((LOCAL, FF), bf16),
            jax.ShapeDtypeStruct((BLOCK, D), bf16),
            jax.ShapeDtypeStruct((BLOCK, D), bf16),
            jax.ShapeDtypeStruct((BLOCK, D), bf16),
            jax.ShapeDtypeStruct((BLOCK, QUARTER), bf16),
        ],
        in_specs=[anywhere] * 3 + [vmem] * 4,
        out_specs=[anywhere] * 2 + [vmem] * 4,
        scratch_shapes=[
            pltpu.VMEM((LOCAL, FF), bf16),
            pltpu.VMEM((LOCAL, D), bf16),
            pltpu.VMEM((LOCAL, D), bf16),
            pltpu.VMEM((4, 4, 4, BLOCK, D), bf16),
            pltpu.VMEM((2, n, 16, 2, ROWS, LOCAL), bf16),
            pltpu.VMEM((n, 16, 2, ROWS, LOCAL), bf16),
            pltpu.VMEM((n, 4, 4, 2 * ROWS, D), f32),
            step1, step1, step1,
            pltpu.VMEM((n, 2, 4, 2 * ROWS, HALF), f32),
            step2, step2, step2,
            pltpu.VMEM((n, 2, ROWS, D), f32),
            pltpu.VMEM((n, ROWS, D), f32),
            pltpu.VMEM((n, ROWS, D), f32),
            pltpu.VMEM((n, 3, ROWS, QUARTER), f32),
            pltpu.VMEM((n, ROWS, D), bf16),
            pltpu.VMEM((LOCAL, D), bf16),
            pltpu.VMEM((LOCAL, FF), bf16),
            dma((3,)),
            dma((2, 4)),
            *pair(3),
            *pair(4, 4, 2, 2),
            *pair(n + 1),
            *pair(n, 3, 2, 2),
            *pair(n, 3, 2, 2),
            *pair(n),
            *pair(n, 3),
            *pair(n, 3),
        ],
        compiler_params=pltpu.CompilerParams(
            collective_id=0, has_side_effects=True, vmem_limit_bytes=60 * MIB
        ),
        cost_estimate=pl.CostEstimate(flops=13 * 10**9, bytes_accessed=13 * MIB, transcendentals=0),
        name="step",
    )(hidden_rows[0], out_grad[0], params[0], first_moment[0], second_moment[0], anchor, outer_momentum)
    return (out[0][None], out[1][None], out[2], out[3][None], out[4][None], out[5])


def solution(mesh):
    rows = P("group", "fsdp", None)
    return jax.shard_map(
        local,
        mesh=mesh,
        in_specs=(rows, rows, rows, rows, rows, P("fsdp", "group"), P("fsdp", "group")),
        out_specs=(rows, rows, P("fsdp", None), rows, rows, P("fsdp", "group")),
        check_vma=False,
    )
```

time: 878 us -> 156 us (0.18)
  waiting for transfers between devices: 819 us -> 0 us
  Pallas kernels: 0 us -> 144 us
  matrix products: 29.9 us -> 0 us
  between operations: 13.8 us -> 0.65 us
  blocking collectives: 9.94 us -> 0 us
    reduce_scatter x2 -> x0, waiting for transfers between devices: 488 us -> none  [the longest x1 419 us: local(): lax.psum_scatter(lax.dot_general(columns, cotangent, (((0,), (0,)), ((),...]
    all_gather x1 -> x0, waiting for transfers between devices: 331 us -> none  [local(): lax.all_gather(weight, 'fsdp', axis=0, tiled=True)]
    pallas_call x0 -> x1, Pallas kernels: none -> 144 us  [local(): pl.pallas_call(kernel, out_shape=[jax.ShapeDtypeStruct((LOCAL, D), bf16),...]
    dot_general x3 -> x0, matrix products: 29.9 us -> none  [the longest x1 10.3 us: local(): lax.dot_general(columns, cotangent, (((0,), (0,)), ((), ())), preferred_e...]
    all_gather x1 -> x0, blocking collectives: 9.94 us -> none  [local(): new_params = lax.all_gather(new_share, 'group', axis=1, tiled=True)]
  transfers between devices with their start and end apart: 3 -> 0, of which waited for: 3 -> 0; matrix products, arithmetic and copies ran while one was open for 3% -> 0% of each run, Pallas kernels for 0% -> 0%
where the time goes in v1:
time: 156 us; the launch traced here: 154 us
  Pallas kernels  144 us (92%)
  local copies, waits for them, and re-layouts  9.61 us (6%)
    pallas_call x1, Pallas kernels, local(): pl.pallas_call(kernel, out_shape=[jax.ShapeDtypeStruct((LOCAL, D), bf16),...  144 us
    unnamed x14, local copies, waits for them, and re-layouts  9.61 us

profile of v1, /device:TPU:1, one launch (start us, length us, event | category | flops | bytes accessed | tf_op | source)
XLA Modules:
  0.0 154.0 jit_solution(13948452072911133380)
XLA Ops:
  0.6 143.7 %step.1 = (bf16[512,1024]{1,0:T(8,128)(2,1)}, bf16[512,4096]{1,0:T(8,128)(2,1)}, bf16[64,1024]{1,0:T(8,128)(2,1)}, bf16[64,1024]{1,0:T(8,128)(2,1)}, bf16[64,1024]{1,0:T(8,128)(2,1)}, /*index=5*/bf16[64,256]{1,0:T(8,128)(2,1)}) custom-call(bf16[512,4096]{1,0:T(8,128)(2,1)} %bitcast.13, bf16[512,1024]{1,0:T(8,128)(2,1)} %bitcast.14, ...), custom_call_target="tpu_custom_call" | custom-call | flops 12999999488 | bytes 13631488 | tf_op jit(solution)/shard_map/step/pallas_call | solution.py:395
  144.4 2.3 %copy.19 = bf16[1,512,1024]{2,1,0:T(8,128)(2,1)} copy(bf16[1,512,1024]{2,1,0:T(8,128)(2,1)} %bitcast.10) | data formatting | bytes 2097152
  146.6 0.0 copy-start.2
  146.6 0.0 copy-start.1
  146.6 0.0 copy-start
  146.6 0.0 copy-start.3
  146.6 4.7 %copy.20 = bf16[1,512,4096]{2,1,0:T(8,128)(2,1)} copy(bf16[1,512,4096]{2,1,0:T(8,128)(2,1)} %bitcast.9) | data formatting | bytes 8388608
  151.4 0.0 copy-done.2
  151.4 0.7 copy.21
  152.0 0.0 copy-done.1
  152.0 0.7 copy.22
  152.7 0.0 copy-done
  152.7 0.7 copy.23
  153.4 0.0 copy-done.3
  153.4 0.6 copy.24
Async XLA Ops:
  146.6 4.8 %copy-start.2 = (bf16[64,1024]{1,0:T(8,128)(2,1)S(1)}, bf16[64,1024]{1,0:T(8,128)(2,1)}, u32[]{:S(2)}) copy-start(bf16[64,1024]{1,0:T(8,128)(2,1)} %get-tuple-element.26) | copy-start | bytes 393220
  146.6 5.4 %copy-start.1 = (bf16[64,1024]{1,0:T(8,128)(2,1)S(1)}, bf16[64,1024]{1,0:T(8,128)(2,1)}, u32[]{:S(2)}) copy-start(bf16[64,1024]{1,0:T(8,128)(2,1)} %get-tuple-element.15) | copy-start | bytes 393220
  146.6 6.1 %copy-start = (bf16[64,1024]{1,0:T(8,128)(2,1)S(1)}, bf16[64,1024]{1,0:T(8,128)(2,1)}, u32[]{:S(2)}) copy-start(bf16[64,1024]{1,0:T(8,128)(2,1)} %get-tuple-element.16) | copy-start | bytes 393220
  146.6 6.7 %copy-start.3 = (bf16[64,256]{1,0:T(8,128)(2,1)S(1)}, bf16[64,256]{1,0:T(8,128)(2,1)}, u32[]{:S(2)}) copy-start(bf16[64,256]{1,0:T(8,128)(2,1)} %get-tuple-element.29) | copy-start | bytes 98308

commit v2 on v1

--- a/solution.py
+++ b/solution.py
@@ -30,10 +30,12 @@
 
 def kernel(
     h_hbm, g_hbm, w_hbm, fm, sm, an, om,
-    lo_hbm, ig_hbm, np_out, nf_out, ns_out, nm_out,
-    h, g, gr, wf, ht, htr, part, o1, n1, s1, sums, o2, n2, s2, plane, zin, inner, gin, share, lo, ig,
-    in_sem, out_sem,
-    wz_ss, wz_rs, ag_ss, ag_rs, ex_ss, ex_rs, r1_ss, r1_rs, r2_ss, r2_rs, zz_ss, zz_rs, gi_ss, gi_rs, np_ss, np_rs,
+    lo, ig, np_out, nf_out, ns_out, nm_out,
+    h, g, gr, wf, ht, htr, part, o1, n1, s1, sums, o2, n2, s2, plane, zin,
+    inner, inner_in, both_sum, both_in, anchors, momenta, moved, share,
+    in_sem,
+    wz_ss, wz_rs, ag_ss, ag_rs, ex_ss, ex_rs, r1_ss, r1_rs, r2_ss, r2_rs, zz_ss, zz_rs,
+    am_ss, am_rs, gi_ss, gi_rs, gh_ss, gh_rs, np_ss, np_rs,
 ):
     me = lax.axis_index("fsdp")
     grp = lax.axis_index("group")
@@ -48,11 +50,9 @@
             return at(lax.rem(x + step + 4, 4), y, z)
         return at(x, lax.rem(y + step + 4, 4), z)
 
-    def peer(e):
-        core, high = lax.rem(grp, 2), grp // 2
-        core = 1 - core if e & 1 else core
-        high = 1 - high if e & 2 else high
-        return high * 2 + core
+    core, high = lax.rem(grp, 2), grp // 2
+    other_core = {"group": high * 2 + 1 - core}
+    other_half = {"group": (1 - high) * 2 + core}
 
     def copy(src, dst, ss, rs, device):
         return pltpu.make_async_remote_copy(
@@ -73,7 +73,7 @@
     barrier = pltpu.get_barrier_semaphore()
     others = [near(a, s) for a in (0, 1) for s in steps]
     others += [at(x, y, lax.rem(z + r, 4)) for r in (1, 2, 3)]
-    others += [{"group": peer(e)} for e in (1, 2, 3)]
+    others += [other_core, other_half]
     for other in others:
         pl.semaphore_signal(barrier, inc=1, device_id=other, device_id_type=pl.DeviceIdType.MESH)
     pl.semaphore_wait(barrier, len(others))
@@ -143,16 +143,21 @@
     def send_z(k):
         return copy(plane.at[k, 1 - level], zin.at[k], zz_ss.at[k], zz_rs.at[k], zcross)
 
-    def send_inner(k, e):
-        other = peer(e)
-        return copy(
-            inner.at[k, :, pl.ds(pl.multiple_of(other * QUARTER, QUARTER), QUARTER)],
-            gin.at[k, e - 1], gi_ss.at[k, e - 1], gi_rs.at[k, e - 1], {"group": other},
-        )
-
-    def send_share(k, e):
-        ref = share.at[k, :, pl.ds(pl.multiple_of(grp * QUARTER, QUARTER), QUARTER)]
-        return copy(ref, ref, np_ss.at[k, e - 1], np_rs.at[k, e - 1], {"group": peer(e)})
+    def send_anchor():
+        return copy(an, anchors.at[high], am_ss.at[0], am_rs.at[0], other_half)
+
+    def send_momentum():
+        return copy(om, momenta.at[high], am_ss.at[1], am_rs.at[1], other_half)
+
+    def send_inner(k):
+        return copy(inner.at[k, :, 1 - core], inner_in.at[k], gi_ss.at[k], gi_rs.at[k], other_core)
+
+    def send_both(k):
+        return copy(both_sum.at[k], both_in.at[k], gh_ss.at[k], gh_rs.at[k], other_half)
+
+    def send_share(k):
+        ref = share.at[k, :, core]
+        return copy(ref, ref, np_ss.at[k], np_rs.at[k], other_core)
 
     both = [(hf, i) for hf in (0, 1) for i in (0, 1)]
 
@@ -237,44 +242,38 @@
         weight = wf[y, x, z, rows, :].astype(f32)
         nf_out[rows, :] = first.astype(bf16)
         ns_out[rows, :] = second.astype(bf16)
-        inner[k] = weight - learn_rate * (first / (jnp.sqrt(second) + adam_eps) + decay_rate * weight)
-        for e in (1, 2, 3):
-            send_inner(k, e).start()
+        fresh = weight - learn_rate * (first / (jnp.sqrt(second) + adam_eps) + decay_rate * weight)
+        for q in range(4):
+            inner[k, q // 2, q % 2] = fresh[:, q * QUARTER : (q + 1) * QUARTER]
+        send_inner(k).start()
 
     def rg(k):
+        send_inner(k).wait_recv()
+        both_sum[k] = inner[k, :, core] + inner_in[k]
+        send_both(k).start()
+
+    def rh(k):
+        send_both(k).wait_recv()
         rows = pl.ds(pl.multiple_of(k * ROWS, ROWS), ROWS)
-        mine = pl.ds(pl.multiple_of(grp * QUARTER, QUARTER), QUARTER)
-        total = inner[k, :, mine]
-        for e in (1, 2, 3):
-            send_inner(k, e).wait_recv()
-            total += gin[k, e - 1]
-        anchor = an[rows, :].astype(f32)
-        pseudo = anchor - total / 4
-        momentum = outer_beta * om[rows, :].astype(f32) + pseudo
-        nm_out[rows, :] = momentum.astype(bf16)
-        share[k, :, mine] = (anchor - outer_rate * (pseudo + outer_beta * momentum)).astype(bf16)
-        for e in (1, 2, 3):
-            send_share(k, e).start()
-
-    def rh(k):
-        for e in (1, 2, 3):
-            send_share(k, e).wait_recv()
-        np_out[pl.ds(pl.multiple_of(k * ROWS, ROWS), ROWS), :] = share[k]
-
-    def out_lo(n):
-        cols = pl.ds(pl.multiple_of(n * 256, 256), 256)
-        return pltpu.make_async_copy(lo.at[:, cols], lo_hbm.at[:, cols], out_sem.at[0, n])
-
-    def out_ig(n):
-        cols = pl.ds(pl.multiple_of(n * 1024, 1024), 1024)
-        return pltpu.make_async_copy(ig.at[:, cols], ig_hbm.at[:, cols], out_sem.at[1, n])
-
-    def piece(n):
+        anchor = anchors[:, rows].astype(f32)
+        pseudo = anchor - (both_sum[k] + both_in[k]) / 4
+        momentum = outer_beta * momenta[:, rows].astype(f32) + pseudo
+        moved[...] = momentum.astype(bf16)
+        nm_out[rows, :] = moved[high]
+        share[k, :, core] = (anchor - outer_rate * (pseudo + outer_beta * momentum)).astype(bf16)
+        send_share(k).start()
+
+    def ri(k):
+        send_share(k).wait_recv()
+        rows = pl.ds(pl.multiple_of(k * ROWS, ROWS), ROWS)
+        for q in range(4):
+            np_out[rows, q * QUARTER : (q + 1) * QUARTER] = share[k, q // 2, q % 2]
+
+    def forward(n):
         cols = pl.ds(pl.multiple_of(n * 256, 256), 256)
         total = jnp.dot(h[...], wf[:, :, :, :, cols].reshape(FF, 256), preferred_element_type=f32)
         lo[:, cols] = (total * (FF ** (-0.5))).astype(bf16)
-        out_lo(n).start()
-
+    def backward(n):
         @pl.loop(0, 4)
         def _(c):
             units = pl.ds(pl.multiple_of(n * 1024 + c * 256, 256), 256)
@@ -283,10 +282,12 @@
             )
             ig[:, units] = (back * (D ** (-0.5))).astype(bf16)
 
-        out_ig(n).start()
-
-    for r in (1, 2, 3):
+    def shard_in(r):
+        copy(w_hbm, wf.at[y, x, z], wz_ss.at[3 - r], wz_rs.at[3 - r], zpair).wait_recv()
+
+    for r in (1, 3, 2):
         wz(r).start()
+    send_g().start()
     load_w.wait()
     ga(0)
     load_h.wait()
@@ -298,34 +299,40 @@
         for par in (0, 1):
             ht[par, :, d, m] = turned[par * BLOCK : (par + 1) * BLOCK].reshape(CHUNKS, ROWS, LOCAL)
 
+    @pl.loop(0, CHUNKS)
+    def _(k):
+        send_h(k).start()
+
+    send_anchor().start()
+    send_momentum().start()
+    anchors[high] = an[...]
+    momenta[high] = om[...]
+
+    load_g.wait()
     gb(0)
-    send_g().start()
-    load_g.wait()
+    shard_in(1)
+    ga(1)
 
     @pl.loop(0, 4)
     def _(r):
+        gc(r)
+
+        @pl.when(r < 2)
+        def _():
+            shard_in(r + 2)
+            ga(r + 2)
+
         @pl.when(r < 3)
         def _():
-            copy(w_hbm, wf.at[y, x, z], wz_ss.at[2 - r], wz_rs.at[2 - r], zpair).wait_recv()
-            ga(r + 1)
-
-        gc(r)
-        send_h(r).start()
-
-        @pl.when(r < 3)
-        def _():
             gb(r + 1)
-
-        gd(r)
-
-    @pl.loop(0, 4)
-    def _(r):
-        ge(r)
-
-    send_g().wait_recv()
+            gd(r)
 
     @pl.loop(0, CHUNKS + 4)
     def _(t):
+        @pl.when(t == 0)
+        def _():
+            send_g().wait_recv()
+
         @pl.when(t < CHUNKS)
         def _():
             send_h(t).wait_recv()
@@ -333,7 +340,15 @@
 
         @pl.when((t >= 1) & (t < CHUNKS + 1))
         def _():
-            rc(t - 1)
+            rd(t - 1)
+
+        @pl.when(t == 0)
+        def _():
+            gd(3)
+
+            @pl.loop(0, 4)
+            def _(r):
+                ge(r)
 
         @pl.when((t >= 2) & (t < CHUNKS + 2))
         def _():
@@ -341,28 +356,40 @@
 
         @pl.when(t < CHUNKS)
         def _():
-            piece(t)
+            forward(t)
             rb(t)
+            backward(t)
+
+        @pl.when((t >= 2) & (t < CHUNKS + 2))
+        def _():
+            rg(t - 2)
 
         @pl.when((t >= 1) & (t < CHUNKS + 1))
         def _():
-            rd(t - 1)
+            re(t - 1)
+
+        @pl.when(t == 3)
+        def _():
+            send_anchor().wait_recv()
+            send_momentum().wait_recv()
 
         @pl.when((t >= 3) & (t < CHUNKS + 3))
         def _():
-            rg(t - 3)
-
-        @pl.when((t >= 1) & (t < CHUNKS + 1))
-        def _():
-            re(t - 1)
+            rh(t - 3)
+
+        @pl.when(t < CHUNKS)
+        def _():
+            rc(t)
 
         @pl.when(t >= 4)
         def _():
-            rh(t - 4)
+            ri(t - 4)
 
     for r in (1, 2, 3):
         wz(r).wait_send()
     send_g().wait_send()
+    send_anchor().wait_send()
+    send_momentum().wait_send()
 
     @pl.loop(0, 4)
     def _(k):
@@ -374,14 +401,13 @@
                 reduce2(kind, k, hf, i).wait_send()
         send_h(k).wait_send()
         send_z(k).wait_send()
-        for e in (1, 2, 3):
-            send_inner(k, e).wait_send()
-            send_share(k, e).wait_send()
-        out_lo(k).wait()
-        out_ig(k).wait()
+        send_inner(k).wait_send()
+        send_both(k).wait_send()
+        send_share(k).wait_send()
 
 
 def local(hidden_rows, out_grad, params, first_moment, second_moment, anchor, outer_momentum):
+    shapes = [(LOCAL, D), (LOCAL, FF), (BLOCK, D), (BLOCK, D), (BLOCK, D), (BLOCK, QUARTER)]
     anywhere = pl.BlockSpec(memory_space=pl.ANY)
     vmem = pl.BlockSpec(memory_space=pltpu.VMEM)
     dma = pltpu.SemaphoreType.DMA
@@ -389,21 +415,16 @@
     step1 = pltpu.VMEM((n, 2, 2, 2, 2 * ROWS, HALF), f32)
     step2 = pltpu.VMEM((n, 2, 2, ROWS, HALF), f32)
 
+    quarters = pltpu.VMEM((n, 2, ROWS, QUARTER), f32)
+
     def pair(*shape):
         return [dma(shape), dma(shape)]
 
     out = pl.pallas_call(
         kernel,
-        out_shape=[
-            jax.ShapeDtypeStruct((LOCAL, D), bf16),
-            jax.ShapeDtypeStruct((LOCAL, FF), bf16),
-            jax.ShapeDtypeStruct((BLOCK, D), bf16),
-            jax.ShapeDtypeStruct((BLOCK, D), bf16),
-            jax.ShapeDtypeStruct((BLOCK, D), bf16),
-            jax.ShapeDtypeStruct((BLOCK, QUARTER), bf16),
-        ],
+        out_shape=[pltpu.VMEM(shape, bf16) for shape in shapes],
         in_specs=[anywhere] * 3 + [vmem] * 4,
-        out_specs=[anywhere] * 2 + [vmem] * 4,
+        out_specs=[vmem] * 6,
         scratch_shapes=[
             pltpu.VMEM((LOCAL, FF), bf16),
             pltpu.VMEM((LOCAL, D), bf16),
@@ -417,24 +438,26 @@
             step2, step2, step2,
             pltpu.VMEM((n, 2, ROWS, D), f32),
             pltpu.VMEM((n, ROWS, D), f32),
-            pltpu.VMEM((n, ROWS, D), f32),
-            pltpu.VMEM((n, 3, ROWS, QUARTER), f32),
-            pltpu.VMEM((n, ROWS, D), bf16),
-            pltpu.VMEM((LOCAL, D), bf16),
-            pltpu.VMEM((LOCAL, FF), bf16),
+            pltpu.VMEM((n, 2, 2, ROWS, QUARTER), f32),
+            quarters, quarters, quarters,
+            pltpu.VMEM((2, BLOCK, QUARTER), bf16),
+            pltpu.VMEM((2, BLOCK, QUARTER), bf16),
+            pltpu.VMEM((2, ROWS, QUARTER), bf16),
+            pltpu.VMEM((n, 2, 2, ROWS, QUARTER), bf16),
             dma((3,)),
-            dma((2, 4)),
             *pair(3),
             *pair(4, 4, 2, 2),
             *pair(n + 1),
             *pair(n, 3, 2, 2),
             *pair(n, 3, 2, 2),
             *pair(n),
-            *pair(n, 3),
-            *pair(n, 3),
+            *pair(2),
+            *pair(n),
+            *pair(n),
+            *pair(n),
         ],
         compiler_params=pltpu.CompilerParams(
-            collective_id=0, has_side_effects=True, vmem_limit_bytes=60 * MIB
+            collective_id=0, has_side_effects=True, vmem_limit_bytes=50 * MIB
         ),
         cost_estimate=pl.CostEstimate(flops=13 * 10**9, bytes_accessed=13 * MIB, transcendentals=0),
         name="step",

time: 156 us -> 138 us (0.88); the launches traced: 154 us -> 138 us
  Pallas kernels: 144 us -> 132 us
  local copies, waits for them, and re-layouts: 9.61 us -> 5.56 us
    pallas_call x1, Pallas kernels: 144 us -> 132 us  [local(): pl.pallas_call(kernel, out_shape=[pltpu.VMEM(shape, bf16) for shape in sh...]
    unnamed x14 -> x6, local copies, waits for them, and re-layouts: 9.61 us -> 5.56 us
where the time goes in v2:
time: 138 us
  Pallas kernels  132 us (96%)
  local copies, waits for them, and re-layouts  5.56 us (4%)
    pallas_call x1, Pallas kernels, local(): pl.pallas_call(kernel, out_shape=[pltpu.VMEM(shape, bf16) for shape in sh...  132 us
    unnamed x6, local copies, waits for them, and re-layouts  5.56 us

profile of v2, /device:TPU:1, one launch (start us, length us, event | category | flops | bytes accessed | tf_op | source)
XLA Modules:
  0.0 137.9 jit_solution(1617742109731141161)
XLA Ops:
  0.6 131.7 %step.1 = (bf16[512,1024]{1,0:T(8,128)(2,1)S(1)}, bf16[512,4096]{1,0:T(8,128)(2,1)S(1)}, bf16[64,1024]{1,0:T(8,128)(2,1)S(1)}, bf16[64,1024]{1,0:T(8,128)(2,1)S(...) custom-call(bf16[512,4096]{1,0:T(8,128)(2,1)} %bitcast.13, bf16[512,1024]{1,0:T(8,128)(2,1)} %bitcast.14, ...), custom_call_target="tpu_custom_call" | custom-call | flops 12999999488 | bytes 13631488 | tf_op jit(solution)/shard_map/step/pallas_call | solution.py:423
  132.4 1.0 copy.19
  133.3 2.0 %copy.20 = bf16[1,512,4096]{2,1,0:T(8,128)(2,1)} copy(bf16[1,512,4096]{2,1,0:T(8,128)(2,1)S(1)} %bitcast.9) | data formatting | bytes 8388608
  135.4 0.6 copy.24
  136.0 0.7 copy.21
  136.6 0.7 copy.22
  137.3 0.7 copy.23

commit v3 on v2

--- a/solution.py
+++ b/solution.py
@@ -29,9 +29,9 @@
 
 
 def kernel(
-    h_hbm, g_hbm, w_hbm, fm, sm, an, om,
+    h_hbm, g_hbm, w_hbm, fm_hbm, sm_hbm, an_hbm, om_hbm,
     lo, ig, np_out, nf_out, ns_out, nm_out,
-    h, g, gr, wf, ht, htr, part, o1, n1, s1, sums, o2, n2, s2, plane, zin,
+    h, g, fm, sm, gr, wf, ht, htr, part, o1, n1, s1, sums, o2, n2, s2, plane, zin,
     inner, inner_in, both_sum, both_in, anchors, momenta, moved, share,
     in_sem,
     wz_ss, wz_rs, ag_ss, ag_rs, ex_ss, ex_rs, r1_ss, r1_rs, r2_ss, r2_rs, zz_ss, zz_rs,
@@ -69,6 +69,14 @@
     load_w.start()
     load_h.start()
     load_g.start()
+    load_small = [
+        pltpu.make_async_copy(src, dst, in_sem.at[3 + j])
+        for j, (src, dst) in enumerate(
+            ((fm_hbm, fm), (sm_hbm, sm), (an_hbm, anchors.at[high]), (om_hbm, momenta.at[high]))
+        )
+    ]
+    for load in load_small:
+        load.start()
 
     barrier = pltpu.get_barrier_semaphore()
     others = [near(a, s) for a in (0, 1) for s in steps]
@@ -144,10 +152,10 @@
         return copy(plane.at[k, 1 - level], zin.at[k], zz_ss.at[k], zz_rs.at[k], zcross)
 
     def send_anchor():
-        return copy(an, anchors.at[high], am_ss.at[0], am_rs.at[0], other_half)
+        return copy(an_hbm, anchors.at[high], am_ss.at[0], am_rs.at[0], other_half)
 
     def send_momentum():
-        return copy(om, momenta.at[high], am_ss.at[1], am_rs.at[1], other_half)
+        return copy(om_hbm, momenta.at[high], am_ss.at[1], am_rs.at[1], other_half)
 
     def send_inner(k):
         return copy(inner.at[k, :, 1 - core], inner_in.at[k], gi_ss.at[k], gi_rs.at[k], other_core)
@@ -185,19 +193,31 @@
         for hf, i in both:
             gather(3, r, hf, i).wait_recv()
 
-    def ra(k):
+    def own(k):
         @pl.loop(0, D // 256)
         def _(n):
             cols = pl.ds(pl.multiple_of(n * 256, 256), 256)
             mine = ht[parity, k].reshape(32 * ROWS, LOCAL)
-            theirs = htr[k].reshape(32 * ROWS, LOCAL)
             total = jnp.dot(mine, g[:, cols], preferred_element_type=f32)
-            total += jnp.dot(theirs, gr[:, cols], preferred_element_type=f32)
             part[k, :, :, :, cols] = total.reshape(4, 4, 2 * ROWS, 256)
 
-        for kind in (0, 1):
-            for hf, i in both:
-                reduce1(kind, k, hf, i).start()
+    def ra(k):
+        @pl.loop(0, 2)
+        def _(hf):
+            @pl.loop(0, 2)
+            def _(n):
+                cols = pl.ds(pl.multiple_of(hf * HALF + n * 256, 256), 256)
+                theirs = htr[k].reshape(32 * ROWS, LOCAL)
+                total = jnp.dot(theirs, gr[:, cols], preferred_element_type=f32)
+                part[k, :, :, :, cols] += total.reshape(4, 4, 2 * ROWS, 256)
+
+            for half in (0, 1):
+
+                @pl.when(hf == half)
+                def _():
+                    for kind in (0, 1):
+                        for i in (0, 1):
+                            reduce1(kind, k, half, i).start()
 
     def rb(k):
         for hf, i in both:
@@ -290,6 +310,8 @@
     send_g().start()
     load_w.wait()
     ga(0)
+    gb(0)
+    gc(0)
     load_h.wait()
 
     @pl.loop(0, 32)
@@ -305,85 +327,93 @@
 
     send_anchor().start()
     send_momentum().start()
-    anchors[high] = an[...]
-    momenta[high] = om[...]
-
+    for load in load_small:
+        load.wait()
     load_g.wait()
-    gb(0)
     shard_in(1)
     ga(1)
-
-    @pl.loop(0, 4)
+    gb(1)
+
+    @pl.loop(1, 4)
     def _(r):
         gc(r)
 
-        @pl.when(r < 2)
+        @pl.when(r < 3)
         def _():
-            shard_in(r + 2)
-            ga(r + 2)
+            shard_in(r + 1)
+            ga(r + 1)
+
+        gd(r - 1)
 
         @pl.when(r < 3)
         def _():
             gb(r + 1)
-            gd(r)
-
-    @pl.loop(0, CHUNKS + 4)
+
+        own(r - 1)
+
+    send_g().wait_recv()
+
+    last = CHUNKS - 1
+
+    @pl.loop(0, CHUNKS)
     def _(t):
-        @pl.when(t == 0)
-        def _():
-            send_g().wait_recv()
-
-        @pl.when(t < CHUNKS)
-        def _():
-            send_h(t).wait_recv()
-            ra(t)
-
-        @pl.when((t >= 1) & (t < CHUNKS + 1))
+        send_h(t).wait_recv()
+        ra(t)
+
+        @pl.when(t >= 1)
         def _():
             rd(t - 1)
 
         @pl.when(t == 0)
         def _():
             gd(3)
+            own(3)
 
             @pl.loop(0, 4)
             def _(r):
                 ge(r)
 
-        @pl.when((t >= 2) & (t < CHUNKS + 2))
-        def _():
-            rf(t - 2)
-
-        @pl.when(t < CHUNKS)
-        def _():
-            forward(t)
-            rb(t)
-            backward(t)
-
-        @pl.when((t >= 2) & (t < CHUNKS + 2))
-        def _():
-            rg(t - 2)
-
-        @pl.when((t >= 1) & (t < CHUNKS + 1))
+        forward(t)
+        rb(t)
+        backward(t)
+
+        @pl.when(t >= 1)
         def _():
             re(t - 1)
 
-        @pl.when(t == 3)
+        @pl.when(t == last)
         def _():
-            send_anchor().wait_recv()
-            send_momentum().wait_recv()
-
-        @pl.when((t >= 3) & (t < CHUNKS + 3))
-        def _():
-            rh(t - 3)
-
-        @pl.when(t < CHUNKS)
-        def _():
-            rc(t)
-
-        @pl.when(t >= 4)
-        def _():
-            ri(t - 4)
+            @pl.loop(0, last - 1)
+            def _(k):
+                rf(k)
+
+        rc(t)
+
+    @pl.loop(0, last - 1)
+    def _(k):
+        rg(k)
+
+    rd(last)
+    send_anchor().wait_recv()
+    send_momentum().wait_recv()
+    rf(last - 1)
+    re(last)
+    rg(last - 1)
+
+    @pl.loop(0, last - 1)
+    def _(k):
+        rh(k)
+
+    rf(last)
+    rg(last)
+    rh(last - 1)
+
+    @pl.loop(0, last)
+    def _(k):
+        ri(k)
+
+    rh(last)
+    ri(last)
 
     for r in (1, 2, 3):
         wz(r).wait_send()
@@ -423,11 +453,13 @@
     out = pl.pallas_call(
         kernel,
         out_shape=[pltpu.VMEM(shape, bf16) for shape in shapes],
-        in_specs=[anywhere] * 3 + [vmem] * 4,
+        in_specs=[anywhere] * 7,
         out_specs=[vmem] * 6,
         scratch_shapes=[
             pltpu.VMEM((LOCAL, FF), bf16),
             pltpu.VMEM((LOCAL, D), bf16),
+            pltpu.VMEM((BLOCK, D), bf16),
+            pltpu.VMEM((BLOCK, D), bf16),
             pltpu.VMEM((LOCAL, D), bf16),
             pltpu.VMEM((4, 4, 4, BLOCK, D), bf16),
             pltpu.VMEM((2, n, 16, 2, ROWS, LOCAL), bf16),
@@ -444,7 +476,7 @@
             pltpu.VMEM((2, BLOCK, QUARTER), bf16),
             pltpu.VMEM((2, ROWS, QUARTER), bf16),
             pltpu.VMEM((n, 2, 2, ROWS, QUARTER), bf16),
-            dma((3,)),
+            dma((7,)),
             *pair(3),
             *pair(4, 4, 2, 2),
             *pair(n + 1),

time: 138 us -> 136 us (0.986)
  Pallas kernels: 132 us -> 130 us
    pallas_call x1, Pallas kernels: 132 us -> 130 us  [local(): pl.pallas_call(kernel, out_shape=[pltpu.VMEM(shape, bf16) for shape in sh...]
where the time goes in v3:
time: 136 us
  Pallas kernels  130 us (96%)
  local copies, waits for them, and re-layouts  5.56 us (4%)
    pallas_call x1, Pallas kernels, local(): pl.pallas_call(kernel, out_shape=[pltpu.VMEM(shape, bf16) for shape in sh...  130 us
    unnamed x6, local copies, waits for them, and re-layouts  5.56 us

profile of v3, /device:TPU:1, one launch (start us, length us, event | category | flops | bytes accessed | tf_op | source)
XLA Modules:
  0.0 136.0 jit_solution(13727131022387075691)
XLA Ops:
  0.6 129.8 %step.1 = (bf16[512,1024]{1,0:T(8,128)(2,1)S(1)}, bf16[512,4096]{1,0:T(8,128)(2,1)S(1)}, bf16[64,1024]{1,0:T(8,128)(2,1)S(1)}, bf16[64,1024]{1,0:T(8,128)(2,1)S(...) custom-call(bf16[512,4096]{1,0:T(8,128)(2,1)} %bitcast.13, bf16[512,1024]{1,0:T(8,128)(2,1)} %bitcast.14, ...), custom_call_target="tpu_custom_call" | custom-call | flops 12999999488 | bytes 13631488 | tf_op jit(solution)/shard_map/step/pallas_call | solution.py:453
  130.5 1.0 copy.19
  131.5 2.0 %copy.20 = bf16[1,512,4096]{2,1,0:T(8,128)(2,1)} copy(bf16[1,512,4096]{2,1,0:T(8,128)(2,1)S(1)} %bitcast.9) | data formatting | bytes 8388608
  133.5 0.6 copy.24
  134.1 0.7 copy.21
  134.7 0.7 copy.22
  135.4 0.7 copy.23

commit v4 on v3

--- a/solution.py
+++ b/solution.py
@@ -12,6 +12,7 @@
 LOCAL = 512
 CHUNKS = 4
 ROWS = BLOCK // CHUNKS
+LAST = CHUNKS - 1
 HALF = D // 2
 QUARTER = D // 4
 MIB = 1 << 20
@@ -30,11 +31,11 @@
 
 def kernel(
     h_hbm, g_hbm, w_hbm, fm_hbm, sm_hbm, an_hbm, om_hbm,
-    lo, ig, np_out, nf_out, ns_out, nm_out,
-    h, g, fm, sm, gr, wf, ht, htr, part, o1, n1, s1, sums, o2, n2, s2, plane, zin,
+    lo, ig, blocks, nm_out,
+    h, g, fm, sm, gr, wf, ht, htr, part, o1, n1, s1, sums, o2, n2, s2, d2, plane, zin,
     inner, inner_in, both_sum, both_in, anchors, momenta, moved, share,
     in_sem,
-    wz_ss, wz_rs, ag_ss, ag_rs, ex_ss, ex_rs, r1_ss, r1_rs, r2_ss, r2_rs, zz_ss, zz_rs,
+    wz_ss, wz_rs, ag_ss, ag_rs, ex_ss, ex_rs, r1_ss, r1_rs, r2_ss, r2_rs, d2_ss, d2_rs, zz_ss, zz_rs,
     am_ss, am_rs, gi_ss, gi_rs, gh_ss, gh_rs, np_ss, np_rs,
 ):
     me = lax.axis_index("fsdp")
@@ -79,7 +80,7 @@
         load.start()
 
     barrier = pltpu.get_barrier_semaphore()
-    others = [near(a, s) for a in (0, 1) for s in steps]
+    others = [near(a, s) for a in (0, 1) for s in (1, -1, 2)]
     others += [at(x, y, lax.rem(z + r, 4)) for r in (1, 2, 3)]
     others += [other_core, other_half]
     for other in others:
@@ -148,6 +149,11 @@
             src, dst = o2.at[k, hf, i], s2.at[k, hf, i]
         return copy(src, dst, r2_ss.at[k, kind, hf, i], r2_rs.at[k, kind, hf, i], near(1 - hf, step))
 
+    def direct2(hf, j):
+        mine = y if hf == 0 else x
+        dest = lax.rem(mine + j + 1, 4)
+        return copy(sums.at[LAST, hf, dest], d2.at[hf, j], d2_ss.at[hf, j], d2_rs.at[hf, j], near(1 - hf, j + 1))
+
     def send_z(k):
         return copy(plane.at[k, 1 - level], zin.at[k], zz_ss.at[k], zz_rs.at[k], zcross)
 
@@ -226,16 +232,34 @@
             o1[k, hf, i] = o1[k, hf, i] + chunk1(k, hf, lax.rem(mine + steps[i] + 4, 4), i)[...]
             reduce1(2, k, hf, i).start()
 
+    def sum1(k, hf):
+        mine = x if hf == 0 else y
+        for i in (0, 1):
+            reduce1(1, k, hf, 1 - i).wait_recv()
+            reduce1(2, k, hf, i).wait_recv()
+            sums[k, hf, pl.ds(2 * i, 2)] = (chunk1(k, hf, mine, i)[...] + s1[k, hf, i]) + n1[k, hf, 1 - i]
+
     def rc(k):
         for hf in (0, 1):
-            mine = x if hf == 0 else y
-            for i in (0, 1):
-                reduce1(1, k, hf, 1 - i).wait_recv()
-                reduce1(2, k, hf, i).wait_recv()
-                sums[k, hf, pl.ds(2 * i, 2)] = (chunk1(k, hf, mine, i)[...] + s1[k, hf, i]) + n1[k, hf, 1 - i]
-        for kind in (0, 1):
-            for hf, i in both:
-                reduce2(kind, k, hf, i).start()
+            sum1(k, hf)
+            for kind in (0, 1):
+                for i in (0, 1):
+                    reduce2(kind, k, hf, i).start()
+
+    def rc_last():
+        for hf in (0, 1):
+            sum1(LAST, hf)
+            for j in (1, 0, 2):
+                direct2(hf, j).start()
+
+    def re_last():
+        for hf in (0, 1):
+            mine = y if hf == 0 else x
+            for j in (0, 2, 1):
+                direct2(hf, j).wait_recv()
+            total = (sums[LAST, hf, mine] + d2[hf, 0]) + (d2[hf, 1] + d2[hf, 2])
+            plane[LAST, :, :, pl.ds(hf * HALF, HALF)] = total.reshape(2, ROWS, HALF)
+        send_z(LAST).start()
 
     def rd(k):
         for hf, i in both:
@@ -260,8 +284,8 @@
         first = beta_first * fm[rows, :].astype(f32) + (1.0 - beta_first) * grad
         second = beta_second * sm[rows, :].astype(f32) + (1.0 - beta_second) * grad * grad
         weight = wf[y, x, z, rows, :].astype(f32)
-        nf_out[rows, :] = first.astype(bf16)
-        ns_out[rows, :] = second.astype(bf16)
+        blocks[1, rows, :] = first.astype(bf16)
+        blocks[2, rows, :] = second.astype(bf16)
         fresh = weight - learn_rate * (first / (jnp.sqrt(second) + adam_eps) + decay_rate * weight)
         for q in range(4):
             inner[k, q // 2, q % 2] = fresh[:, q * QUARTER : (q + 1) * QUARTER]
@@ -287,7 +311,7 @@
         send_share(k).wait_recv()
         rows = pl.ds(pl.multiple_of(k * ROWS, ROWS), ROWS)
         for q in range(4):
-            np_out[rows, q * QUARTER : (q + 1) * QUARTER] = share[k, q // 2, q % 2]
+            blocks[0, rows, q * QUARTER : (q + 1) * QUARTER] = share[k, q // 2, q % 2]
 
     def forward(n):
         cols = pl.ds(pl.multiple_of(n * 256, 256), 256)
@@ -302,10 +326,21 @@
             )
             ig[:, units] = (back * (D ** (-0.5))).astype(bf16)
 
+    def sent1(k):
+        for hf, i in both:
+            for kind in range(3):
+                reduce1(kind, k, hf, i).wait_send()
+        send_h(k).wait_send()
+
+    def sent2(k):
+        for hf, i in both:
+            for kind in range(3):
+                reduce2(kind, k, hf, i).wait_send()
+
     def shard_in(r):
         copy(w_hbm, wf.at[y, x, z], wz_ss.at[3 - r], wz_rs.at[3 - r], zpair).wait_recv()
 
-    for r in (1, 3, 2):
+    for r in (3, 2, 1):
         wz(r).start()
     send_g().start()
     load_w.wait()
@@ -353,16 +388,22 @@
 
     send_g().wait_recv()
 
-    last = CHUNKS - 1
-
     @pl.loop(0, CHUNKS)
     def _(t):
+        for hf, i in both:
+            for kind in range(4):
+                gather(kind, t, hf, i).wait_send()
+
+        @pl.when(t >= 1)
+        def _():
+            sent1(t - 1)
+
+        @pl.when(t >= 2)
+        def _():
+            sent2(t - 2)
+
         send_h(t).wait_recv()
         ra(t)
-
-        @pl.when(t >= 1)
-        def _():
-            rd(t - 1)
 
         @pl.when(t == 0)
         def _():
@@ -373,71 +414,83 @@
             def _(r):
                 ge(r)
 
+        @pl.when(t >= 2)
+        def _():
+            re(t - 2)
+
         forward(t)
+
+        @pl.when(t >= 1)
+        def _():
+            rc(t - 1)
+
         rb(t)
+
+        @pl.when(t >= 1)
+        def _():
+            rd(t - 1)
+
         backward(t)
 
-        @pl.when(t >= 1)
-        def _():
-            re(t - 1)
-
-        @pl.when(t == last)
-        def _():
-            @pl.loop(0, last - 1)
-            def _(k):
-                rf(k)
-
-        rc(t)
-
-    @pl.loop(0, last - 1)
+    re(LAST - 1)
+
+    @pl.loop(0, LAST - 1)
+    def _(k):
+        rf(k)
+
+    rc_last()
+    rf(LAST - 1)
+
+    @pl.loop(0, LAST - 1)
     def _(k):
         rg(k)
 
-    rd(last)
     send_anchor().wait_recv()
     send_momentum().wait_recv()
-    rf(last - 1)
-    re(last)
-    rg(last - 1)
-
-    @pl.loop(0, last - 1)
+    re_last()
+    rg(LAST - 1)
+
+    @pl.loop(0, LAST - 1)
     def _(k):
         rh(k)
 
-    rf(last)
-    rg(last)
-    rh(last - 1)
-
-    @pl.loop(0, last)
+    rf(LAST)
+    rg(LAST)
+    rh(LAST - 1)
+
+    @pl.loop(0, LAST)
     def _(k):
         ri(k)
-
-    rh(last)
-    ri(last)
 
     for r in (1, 2, 3):
         wz(r).wait_send()
     send_g().wait_send()
     send_anchor().wait_send()
     send_momentum().wait_send()
-
-    @pl.loop(0, 4)
-    def _(k):
-        for hf, i in both:
-            for kind in range(4):
-                gather(kind, k, hf, i).wait_send()
-            for kind in range(3):
-                reduce1(kind, k, hf, i).wait_send()
-                reduce2(kind, k, hf, i).wait_send()
-        send_h(k).wait_send()
+    sent1(LAST)
+    sent2(LAST - 1)
+    for hf in (0, 1):
+        for j in range(3):
+            direct2(hf, j).wait_send()
+
+    @pl.loop(0, CHUNKS)
+    def _(k):
         send_z(k).wait_send()
         send_inner(k).wait_send()
+
+    @pl.loop(0, LAST)
+    def _(k):
         send_both(k).wait_send()
         send_share(k).wait_send()
 
+    rh(LAST)
+    ri(LAST)
+    send_both(LAST).wait_send()
+    send_share(LAST).wait_send()
+
 
 def local(hidden_rows, out_grad, params, first_moment, second_moment, anchor, outer_momentum):
-    shapes = [(LOCAL, D), (LOCAL, FF), (BLOCK, D), (BLOCK, D), (BLOCK, D), (BLOCK, QUARTER)]
+    shapes = [(LOCAL, D), (LOCAL, FF), (3, BLOCK, D), (BLOCK, QUARTER)]
     anywhere = pl.BlockSpec(memory_space=pl.ANY)
     vmem = pl.BlockSpec(memory_space=pltpu.VMEM)
     dma = pltpu.SemaphoreType.DMA
@@ -454,7 +507,7 @@
         kernel,
         out_shape=[pltpu.VMEM(shape, bf16) for shape in shapes],
         in_specs=[anywhere] * 7,
-        out_specs=[vmem] * 6,
+        out_specs=[vmem] * 4,
         scratch_shapes=[
             pltpu.VMEM((LOCAL, FF), bf16),
             pltpu.VMEM((LOCAL, D), bf16),
@@ -468,6 +521,7 @@
             step1, step1, step1,
             pltpu.VMEM((n, 2, 4, 2 * ROWS, HALF), f32),
             step2, step2, step2,
+            pltpu.VMEM((2, 3, 2 * ROWS, HALF), f32),
             pltpu.VMEM((n, 2, ROWS, D), f32),
             pltpu.VMEM((n, ROWS, D), f32),
             pltpu.VMEM((n, 2, 2, ROWS, QUARTER), f32),
@@ -482,6 +536,7 @@
             *pair(n + 1),
             *pair(n, 3, 2, 2),
             *pair(n, 3, 2, 2),
+            *pair(2, 3),
             *pair(n),
             *pair(2),
             *pair(n),
@@ -494,7 +549,7 @@
         cost_estimate=pl.CostEstimate(flops=13 * 10**9, bytes_accessed=13 * MIB, transcendentals=0),
         name="step",
     )(hidden_rows[0], out_grad[0], params[0], first_moment[0], second_moment[0], anchor, outer_momentum)
-    return (out[0][None], out[1][None], out[2], out[3][None], out[4][None], out[5])
+    return (out[0][None], out[1][None], out[2][0], out[2][1:2], out[2][2:3], out[3])
 
 
 def solution(mesh):

time: 136 us -> 132 us (0.971)
  Pallas kernels: 130 us -> 127 us
    pallas_call x1, Pallas kernels: 130 us -> 127 us  [local(): pl.pallas_call(kernel, out_shape=[pltpu.VMEM(shape, bf16) for shape in sh...]
    unnamed x6 -> x3, local copies, waits for them, and re-layouts: 5.56 us -> 3.6 us
where the time goes in v4:
time: 132 us
  Pallas kernels  127 us (96%)
  local copies, waits for them, and re-layouts  4.35 us (3%)
    pallas_call x1, Pallas kernels, local(): pl.pallas_call(kernel, out_shape=[pltpu.VMEM(shape, bf16) for shape in sh...  127 us
    unnamed x3, local copies, waits for them, and re-layouts  3.6 us

profile of v4, /device:TPU:1, one launch (start us, length us, event | category | flops | bytes accessed | tf_op | source)
XLA Modules:
  0.0 132.3 jit_solution(5494713337410787895)
XLA Ops:
  0.6 127.3 %step.1 = (bf16[512,1024]{1,0:T(8,128)(2,1)S(1)}, bf16[512,4096]{1,0:T(8,128)(2,1)S(1)}, bf16[3,64,1024]{2,1,0:T(8,128)(2,1)S(1)}, bf16[64,256]{1,0:T(8,128)(2,1)S(1)}) custom-call(bf16[512,4096]{1,0:T(8,128)(2,1)} %bitcast.11, bf16[512,1024]{1,0:T(8,128)(2,1)} %bitcast.12, bf16[64,1024]{1,0:T(8,128)(2,1)} %bitcast.13, bf16[64,1024]{1,0:T(8,128)(2,1)} %bitcast.14, ...), custom_call_target="tpu_custom_call" | custom-call | flops 12999999488 | bytes 13631488 | tf_op jit(solution)/shard_map/step/pallas_call | solution.py:506
  128.0 1.0 copy.16
  129.0 2.0 %copy.17 = bf16[1,512,4096]{2,1,0:T(8,128)(2,1)} copy(bf16[1,512,4096]{2,1,0:T(8,128)(2,1)S(1)} %bitcast.9) | data formatting | bytes 8388608
  131.0 0.6 copy.18
  131.6 0.7 fusion

commit v5 on v4

--- a/solution.py
+++ b/solution.py
@@ -163,6 +163,11 @@
     def send_momentum():
         return copy(om_hbm, momenta.at[high], am_ss.at[1], am_rs.at[1], other_half)
 
+    def send_z_half(hf):
+        cols = pl.ds(hf * HALF, HALF)
+        src, dst = plane.at[LAST, 1 - level, :, cols], zin.at[LAST, :, cols]
+        return copy(src, dst, zz_ss.at[LAST + hf], zz_rs.at[LAST + hf], zcross)
+
     def send_inner(k):
         return copy(inner.at[k, :, 1 - core], inner_in.at[k], gi_ss.at[k], gi_rs.at[k], other_core)
 
@@ -258,8 +263,9 @@
             for j in (0, 2, 1):
                 direct2(hf, j).wait_recv()
             total = (sums[LAST, hf, mine] + d2[hf, 0]) + (d2[hf, 1] + d2[hf, 2])
-            plane[LAST, :, :, pl.ds(hf * HALF, HALF)] = total.reshape(2, ROWS, HALF)
-        send_z(LAST).start()
+            cols = pl.ds(hf * HALF, HALF)
+            plane[LAST, :, :, cols] = total.reshape(2, ROWS, HALF)
+            send_z_half(hf).start()
 
     def rd(k):
         for hf, i in both:
@@ -278,7 +284,11 @@
         send_z(k).start()
 
     def rf(k):
-        send_z(k).wait_recv()
+        if isinstance(k, int) and k == LAST:
+            for hf in (0, 1):
+                send_z_half(hf).wait_recv()
+        else:
+            send_z(k).wait_recv()
         rows = pl.ds(pl.multiple_of(k * ROWS, ROWS), ROWS)
         grad = (plane[k, level] + zin[k]) * (TOKENS ** (-0.5))
         first = beta_first * fm[rows, :].astype(f32) + (1.0 - beta_first) * grad
@@ -418,13 +428,12 @@
         def _():
             re(t - 2)
 
+        @pl.when(t >= 1)
+        def _():
+            rc(t - 1)
+
+        rb(t)
         forward(t)
-
-        @pl.when(t >= 1)
-        def _():
-            rc(t - 1)
-
-        rb(t)
 
         @pl.when(t >= 1)
         def _():
@@ -475,11 +484,14 @@
 
     @pl.loop(0, CHUNKS)
     def _(k):
+        send_inner(k).wait_send()
+
+    for hf in (0, 1):
+        send_z_half(hf).wait_send()
+
+    @pl.loop(0, LAST)
+    def _(k):
         send_z(k).wait_send()
-        send_inner(k).wait_send()
-
-    @pl.loop(0, LAST)
-    def _(k):
         send_both(k).wait_send()
         send_share(k).wait_send()
 
@@ -537,7 +549,7 @@
             *pair(n, 3, 2, 2),
             *pair(n, 3, 2, 2),
             *pair(2, 3),
-            *pair(n),
+            *pair(n + 1),
             *pair(2),
             *pair(n),
             *pair(n),

time: 132 us -> 132 us (level)
  no operation moved by 1% of the time
where the time goes in v5:
time: 132 us
  Pallas kernels  127 us (96%)
  local copies, waits for them, and re-layouts  4.35 us (3%)
    pallas_call x1, Pallas kernels, local(): pl.pallas_call(kernel, out_shape=[pltpu.VMEM(shape, bf16) for shape in sh...  127 us
    unnamed x3, local copies, waits for them, and re-layouts  3.6 us

profile of v5, /device:TPU:1, one launch (start us, length us, event | category | flops | bytes accessed | tf_op | source)
XLA Modules:
  0.0 131.7 jit_solution(263886788662441195)
XLA Ops:
  0.6 126.7 %step.1 = (bf16[512,1024]{1,0:T(8,128)(2,1)S(1)}, bf16[512,4096]{1,0:T(8,128)(2,1)S(1)}, bf16[3,64,1024]{2,1,0:T(8,128)(2,1)S(1)}, bf16[64,256]{1,0:T(8,128)(2,1)S(1)}) custom-call(bf16[512,4096]{1,0:T(8,128)(2,1)} %bitcast.11, bf16[512,1024]{1,0:T(8,128)(2,1)} %bitcast.12, bf16[64,1024]{1,0:T(8,128)(2,1)} %bitcast.13, bf16[64,1024]{1,0:T(8,128)(2,1)} %bitcast.14, ...), custom_call_target="tpu_custom_call" | custom-call | flops 12999999488 | bytes 13631488 | tf_op jit(solution)/shard_map/step/pallas_call | solution.py:518
  127.3 1.0 copy.16
  128.3 2.0 %copy.17 = bf16[1,512,4096]{2,1,0:T(8,128)(2,1)} copy(bf16[1,512,4096]{2,1,0:T(8,128)(2,1)S(1)} %bitcast.9) | data formatting | bytes 8388608
  130.3 0.6 copy.18
  130.9 0.7 fusion
